TPU v7x, 512 devices: a whole 4x4x16 slice. The times are simulated.
512 devices in a mesh: virt: 32 (over y_lo, z), ao: 16 (over y_hi, x, core).
Axes of the slice: x: 4, y: 4 (y_hi: 2, y_lo: 2; y = y_hi * 2 + y_lo), z: 16, core: 2. Of those that a mesh axis runs over, the one named last changes fastest.
Arguments:
- density: bfloat16 [640, 640, 128], P('virt', 'ao'), may hold values from -6 to 6
- virt_coeff: bfloat16 [640, 1024], P('virt'), may hold values from -0.25 to 0.25
- block_coeff: bfloat16 [128, 1024], P('ao'), may hold values from -0.5 to 0.5
- ao_order: int32 [1024], replicated, may hold values from 0 to 1023, each once
Outputs:
- density_ao: bfloat16 [1024, 1024, 1024], P('ao', 'virt')
Inputs may be any that keep to these rules, and one draw needn't show every extreme that they name: `ao_order`: each basis function appears exactly once.
All inputs are finite; a program needn't handle non-finite values.
Results may differ from a plain program's by a relative error of at most 0.0057.
Values may be sent and summed in bfloat16 or wider, within the bound.
A program may use at most 64 MiB of HBM per device.

v0:
```python
import jax
import jax.numpy as jnp
from jax import lax
from jax.sharding import PartitionSpec as P


def shards(density, virt_coeff, block_coeff, ao_order):
    coeff_all = lax.all_gather(virt_coeff, "virt", axis=0, tiled=True)
    whole_block = lax.all_gather(block_coeff, "ao", axis=0, tiled=True)
    coef_panel = jnp.take(whole_block, ao_order, axis=1)
    quarter = jnp.einsum(
        "abc,cs->abs", density, coef_panel, preferred_element_type=jnp.float32
    ).astype(jnp.bfloat16)
    halfway = jnp.einsum(
        "abs,bn->asn",
        lax.all_to_all(quarter, "ao", split_axis=2, concat_axis=1, tiled=True),
        coeff_all,
        preferred_element_type=jnp.float32,
    ).astype(jnp.bfloat16)
    return jnp.einsum(
        "asn,am->snm",
        lax.all_to_all(halfway, "virt", split_axis=2, concat_axis=0, tiled=True),
        coeff_all,
        preferred_element_type=jnp.float32,
    ).astype(jnp.bfloat16)


def solution(mesh):
    return jax.shard_map(
        shards,
        mesh=mesh,
        in_specs=(P("virt", "ao", None), P("virt", None), P("ao", None), P()),
        out_specs=P("ao", "virt", None),
        check_vma=False,
    )
```

profile of v0, /device:TPU:4, one launch (start us, length us, event | category | flops | bytes accessed | tf_op | source)
XLA Modules:
  0.0 316.3 jit_solution(8852735549758202453)
XLA Ops:
  6.5 0.0 copy-start
  6.5 0.0 all-gather.3.cloned.1.call-start
  6.5 0.7 all-gather.3.cloned.1.call-update
  7.3 20.8 %all_gather.6 = bf16[128,1024]{1,0:T(8,128)(2,1)S(1)} all-gather(bf16[8,1024]{1,0:T(8,128)(2,1)} %param.6), channel_id=1, replica_groups=mesh['virt'=32,'ao'=16] {'ao'}, dimensions={0}, use_global_device_ids=true | all-gather | bytes 278528 | tf_op jit(solution)/shard_map/all_gather | solution.py:9
  28.0 0.2 copy.14
  28.2 0.7 fusion.5
  28.9 3.2 %gather_fusion = bf16[1024,128]{1,0:T(8,128)(2,1)S(1)} fusion(bf16[128,1024]{0,1:T(8,128)(2,1)S(1)} %copy.14, s32[1024]{0:T(1024)S(1)} %fusion.5), kind=kCustom, calls=%fused_computation | custom fusion | bytes 528384 | tf_op jit(solution)/shard_map/jit(_take)/gather | solution.py:10
  32.1 0.0 copy-done.2
  32.2 0.7 fusion
  32.9 6.3 %copy.15 = bf16[20,40,1024]{1,0,2:T(8,128)(2,1)} copy(bf16[20,40,1024]{2,1,0:T(8,128)(2,1)S(1)} %fusion) | data formatting | bytes 3276800 | tf_op jit(solution)/shard_map/convert_element_type | solution.py:13
  39.2 9.2 %reshape.19 = bf16[16,2,25600]{2,1,0:T(2,128)(2,1)S(1)} reshape(bf16[1024,20,40]{2,1,0:T(8,128)(2,1)} %bitcast.25) | data formatting | bytes 3276800
  48.4 32.9 %all_to_all.36 = bf16[16,2,25600]{2,1,0:T(2,128)(2,1)S(1)} all-to-all(bf16[16,2,25600]{2,1,0:T(2,128)(2,1)S(1)} %reshape.19), channel_id=1, replica_groups=mesh['virt'=32,'ao'=16] {'ao'}, dimensions={0} | all-to-all | bytes 3276800 | tf_op jit(solution)/shard_map/all_to_all | solution.py:16
  81.3 8.4 %reshape.20 = bf16[1024,20,40]{2,1,0:T(8,128)(2,1)} reshape(bf16[16,2,25600]{2,1,0:T(2,128)(2,1)S(1)} %all_to_all.36) | data formatting | bytes 3276800
  89.6 6.6 %copy.16 = bf16[20,40,16,64]{3,1,2,0:T(8,128)(2,1)S(1)} copy(bf16[20,40,16,64]{1,0,3,2:T(8,128)(2,1)} %bitcast.23) | data formatting | bytes 3276800 | tf_op jit(solution)/shard_map/all_to_all | solution.py:16
  96.3 51.5 %all-gather.3.cloned.1.call-done = bf16[32,20,1024]{2,1,0:T(8,128)(2,1)} async-done(((bf16[1,20,1024]{2,1,0:T(8,128)(2,1)}), bf16[32,20,1024]{2,1,0:T(8,128)(2,1)}) %all-gather.3.cloned.1.call-update) | async-done | bytes 1310736 | tf_op jit(solution)/shard_map/all_gather | solution.py:8
  147.8 3.3 %reshape.17 = bf16[640,1024,1]{1,0,2:T(8,128)(2,1)} reshape(bf16[32,20,1024]{2,1,0:T(8,128)(2,1)} %all-gather.3.cloned.1.call-done) | data formatting | bytes 2621440
  151.1 5.1 %convolution_convert_fusion.1 = bf16[20,64,1024]{2,1,0:T(8,128)(2,1)} fusion(bf16[20,640,64]{2,1,0:T(8,128)(2,1)S(1)} %bitcast.28, bf16[640,1024,1]{1,0,2:T(8,128)(2,1)} %reshape.17), kind=kOutput, calls=%fused_computation.2 | convolution fusion | flops 1679032320 | bytes 5570560 | tf_op jit(solution)/shard_map/abs,bn->asn/dot_general | solution.py:14
  156.2 7.6 %copy.18 = bf16[20,64,1024]{1,0,2:T(8,128)(2,1)} copy(bf16[20,64,1024]{2,1,0:T(8,128)(2,1)} %convolution_convert_fusion.1) | data formatting | bytes 5242880 | tf_op jit(solution)/shard_map/convert_element_type | solution.py:19
  163.8 7.1 %reshape.21 = bf16[32,2,20480]{2,1,0:T(2,128)(2,1)S(1)} reshape(bf16[1024,20,64]{2,1,0:T(8,128)(2,1)} %bitcast.24) | data formatting | bytes 5242880
  170.9 106.4 %all_to_all.37 = bf16[32,2,20480]{2,1,0:T(2,128)(2,1)} all-to-all(bf16[32,2,20480]{2,1,0:T(2,128)(2,1)S(1)} %reshape.21), channel_id=1, replica_groups=mesh['virt'=32,'ao'=16] {'virt'}, dimensions={0} | all-to-all | bytes 5242880 | tf_op jit(solution)/shard_map/all_to_all | solution.py:22
  277.3 9.0 %reshape.22 = bf16[1024,20,64]{2,1,0:T(8,128)(2,1)} reshape(bf16[32,2,20480]{2,1,0:T(2,128)(2,1)} %all_to_all.37) | data formatting | bytes 5242880
  286.2 6.4 %copy.20 = bf16[32,20,64,32]{2,3,1,0:T(8,128)(2,1)} copy(bf16[32,20,64,32]{2,1,3,0:T(8,128)(2,1)} %bitcast.26) | data formatting | bytes 5242880 | tf_op jit(solution)/shard_map/all_to_all | solution.py:22
  292.6 10.1 %copy.21 = bf16[640,64,32]{0,2,1:T(8,128)(2,1)} copy(bf16[640,64,32]{1,2,0:T(8,128)(2,1)} %bitcast.27) | data formatting | bytes 5242880 | tf_op jit(solution)/shard_map/all_to_all | solution.py:22
  302.7 6.7 %convolution_convert_fusion = bf16[64,32,1024]{2,1,0:T(8,128)(2,1)} fusion(bf16[640,64,32]{0,2,1:T(8,128)(2,1)} %copy.21, bf16[640,1024,1]{1,0,2:T(8,128)(2,1)S(1)} %copy-done.1), kind=kOutput, calls=%fused_computation.1 | convolution fusion | flops 2686451712 | bytes 8126464 | tf_op jit(solution)/shard_map/asn,am->snm/dot_general | solution.py:20
  (5 shorter events, 0.0 us)
Async XLA Ops:
  6.5 25.6 %copy-start = (bf16[20,40,128]{2,1,0:T(8,128)(2,1)S(1)}, bf16[20,40,128]{2,1,0:T(8,128)(2,1)}, u32[]{:S(2)}) copy-start(bf16[20,40,128]{2,1,0:T(8,128)(2,1)} %param.4) | copy-start | bytes 614404
  6.5 25.6 %copy-start.2 = (s32[1024]{0:T(1024)S(1)}, s32[1024]{0:T(1024)}, u32[]{:S(2)}) copy-start(s32[1024]{0:T(1024)} %param.7) | copy-start | bytes 12292
  6.5 141.2 %all-gather.3.cloned.1.call-start = ((), (), s32[]{:S(2)}) async-start(), calls=%async_computation.2 | async-start | bytes 1622016 | tf_op jit(solution)/shard_map/all_gather | solution.py:8
  292.6 10.1 %copy-start.1 = (bf16[640,1024,1]{1,0,2:T(8,128)(2,1)S(1)}, bf16[640,1024,1]{1,0,2:T(8,128)(2,1)}, u32[]{:S(2)}) copy-start(bf16[640,1024,1]{1,0,2:T(8,128)(2,1)} %reshape.17) | copy-start | bytes 3932164
Sparse Core Ops, SparseCore 0:
  9.4 138.2 all-gather.2
where the time goes:
time: 317 us; the launch traced here: 316 us
  blocking collectives  160 us (50%)
  local copies, waits for them, and re-layouts  77.4 us (24%)
  waiting for transfers between devices  52.2 us (16%)
  between operations  13.5 us (4%)
  matrix products  12.5 us (4%)
    all_to_all x1, blocking collectives, shards(): lax.all_to_all(halfway, 'virt', split_axis=2, concat_axis=0, tiled=True)  106 us
    all_gather x1, waiting for transfers between devices, shards(): coeff_all = lax.all_gather(virt_coeff, 'virt', axis=0, tiled=True)  51.5 us
    unnamed x11, local copies, waits for them, and re-layouts  36.9 us
    all_to_all x1, blocking collectives, shards(): lax.all_to_all(quarter, 'ao', split_axis=2, concat_axis=1, tiled=True)  32.9 us
    all_gather x1, blocking collectives, shards(): whole_block = lax.all_gather(block_coeff, 'ao', axis=0, tiled=True)  20.8 us
    all_to_all x2, local copies, waits for them, and re-layouts, shards(): lax.all_to_all(halfway, 'virt', split_axis=2, concat_axis=0, tiled=True)  16.5 us
    convert_element_type x1, local copies, waits for them, and re-layouts, shards(): halfway = jnp.einsum('abs,bn->asn', lax.all_to_all(quarter, 'ao', split_a...  7.61 us
    dot_general x1, matrix products, shards(): jnp.einsum('asn,am->snm', lax.all_to_all(halfway, 'virt', split_axis=2, c...  6.68 us
  transfers between devices with their start and end apart: 1, of which 1 were waited for; matrix products, arithmetic and copies ran while one was open for 11% of the time, Pallas kernels for 0%

commit v1 on v0

v1 whole, which is shorter than its diff:
```python
import jax
import jax.numpy as jnp
from jax import lax
from jax.experimental import pallas as pl
from jax.experimental.pallas import tpu as pltpu
from jax.sharding import PartitionSpec as P

MESH = pl.DeviceIdType.MESH
BF = jnp.bfloat16
F32 = jnp.float32
TN = (((0,), (0,)), ((), ()))
NT = (((1,), (1,)), ((), ()))


def exchange(
    order_ref, d_ref, c_ref, b_ref, h_ref, cp_ref,
    dl, cl, bl, hot, pt, df, dp, cf, t1, s, r, rf, g, ta, hf,
    dss, dsr, css, csr, cps, cpr, ccs, ccr, bs, br, zs, zr, ps, pr, qs, qr, ks, kr, ls, lr,
):
    v, j = lax.axis_index("virt"), lax.axis_index("ao")
    y_lo, z = v // 16, v % 16
    core, x, y_hi = j % 2, (j // 2) % 4, j // 8
    y = 2 * y_hi + y_lo
    jc = j // 2
    lanes = pl.ds(pl.multiple_of(jc * 128, 128), 128)
    other = (v, j + 1 - 2 * core)

    def plane(d, sign):
        yy = (y + sign * (d // 4) + 4) % 4
        xx = (x + sign * (d % 4) + 4) % 4
        return yy, xx, (yy % 2) * 16 + z, (yy // 2) * 8 + xx * 2 + core

    def remote(src, dst, send, recv, dev):
        return pltpu.make_async_remote_copy(
            src_ref=src, dst_ref=dst, send_sem=send, recv_sem=recv, device_id=dev, device_id_type=MESH
        )

    barrier = pltpu.get_barrier_semaphore()

    @pl.loop(1, 16)
    def _(t):
        pl.semaphore_signal(barrier, inc=1, device_id=(v, (j + t) % 16), device_id_type=MESH)
        pl.semaphore_signal(barrier, inc=1, device_id=(y_lo * 16 + (z + t) % 16, j), device_id_type=MESH)

    @pl.loop(1, 16)
    def _(t):
        yy, xx, vv, jj = plane(t, 1)

        @pl.when(yy % 2 != y_lo)
        def _():
            pl.semaphore_signal(barrier, inc=1, device_id=(vv, jj), device_id_type=MESH)

    pl.semaphore_wait(barrier, 38)

    def c_z(t):
        return remote(c_ref.at[:, lanes], cl.at[core, y, x, z // 2], css.at[t], csr.at[z // 2],
                      (y_lo * 16 + (z + t) % 16, j))

    @pl.when(z % 2 == core)
    def _():
        @pl.loop(1, 16)
        def _(t):
            c_z(t).start()

        cl[core, y, x, z // 2] = c_ref[:, lanes]

    def d_a(t, u):
        jj = (j + t) % 16
        src = d_ref.at[jj] if u == 0 else d_ref.at[16 + jj // 4]
        return remote(src, dl.at[u, j], dss.at[u, t], dsr.at[u, t], (v, jj))

    @pl.loop(1, 16)
    def _(t):
        d_a(t, 0).start()
        d_a(t, 1).start()

    dl[0, j] = d_ref[j]
    dl[1, j] = d_ref[16 + j // 4]

    @pl.loop(0, 8)
    def _(zz):
        @pl.when(2 * zz + core != z)
        def _():
            remote(c_ref.at[:, lanes], cl.at[core, y, x, zz], css.at[0], csr.at[zz], other).wait_recv()

    def c_p(d, slot_y, slot_x, dev):
        blk = cl.at[core, slot_y, slot_x]
        return remote(blk, blk, cps.at[d], cpr.at[d], dev)

    def c_c(d, k, slot_y, slot_x):
        blk = cl.at[k, slot_y, slot_x]
        return remote(blk, blk, ccs.at[d], ccr.at[d], other)

    @pl.loop(1, 16)
    def _(d):
        yy, xx, vv, jj = plane(d, 1)
        c_p(d, y, x, (vv, jj)).start()

    c_c(0, core, y, x).start()

    def b_a(t):
        return remote(b_ref, bl.at[j], bs.at[t], br.at[t], (v, (j + t) % 16))

    @pl.loop(1, 16)
    def _(t):
        b_a(t).start()

    bl[j] = b_ref[...]

    column = lax.broadcasted_iota(jnp.int32, (1, 1024), 1)

    @pl.loop(0, 64)
    def _(k):
        hot[pl.ds(k, 1), :] = jnp.where(column == order_ref[j * 64 + k], 1.0, 0.0).astype(F32)

    @pl.loop(1, 16)
    def _(t):
        frm = (j - t + 16) % 16
        for u in range(2):
            remote(d_ref.at[0], dl.at[u, frm], dss.at[u, t], dsr.at[u, t], other).wait_recv()

    for u in range(2):
        for jj in range(16):
            df[u, pl.ds(jj * 40, 40), :] = dl[u, jj].astype(F32)
        for q in range(40):
            dp[u, pl.ds(q * 16, 16), :] = df[u, pl.ds((q // 20) * 320 + q % 20, 16, stride=20), :].astype(BF)

    @pl.loop(1, 16)
    def _(d):
        yy, xx, vv, jj = plane(d, -1)
        c_p(d, yy, xx, other).wait_recv()
        c_c(d, core, yy, xx).start()

    @pl.loop(0, 16)
    def _(d):
        yy, xx, vv, jj = plane(d, -1)
        c_c(d, 1 - core, yy, xx).wait_recv()

    @pl.loop(0, 8)
    def _(q):
        xx, yh = q % 4, q // 4
        for yl in range(2):
            for zz in range(16):
                cf[yl * 16 + zz, pl.ds(0, 20), :] = cl[zz % 2, 2 * yh + yl, xx, zz // 2].astype(F32)
        flat = cf.reshape(32 * 24, 128)
        for k in range(40):
            cp_ref[pl.ds(k * 16, 16), pl.ds(pl.multiple_of(q * 128, 128), 128)] = flat[
                pl.ds((k // 20) * 384 + k % 20, 16, stride=24), :
            ].astype(BF)

    @pl.loop(0, 8)
    def _(q):
        yl, z4 = q // 4, (q % 4) * 4
        cols = cp_ref[:, pl.ds(pl.multiple_of(q * 128, 128), 128)]
        for u in range(2):
            tt = lax.dot_general(dp[u], cols, TN, preferred_element_type=F32)
            tt = tt.T.astype(BF)
            for e in range(4):
                if u == 0:
                    s[z4 + e, pl.ds(pl.multiple_of(yl * 32, 32), 32), :] = tt[e * 32:(e + 1) * 32]
                else:
                    t1[yl * 2, z4 + e] = tt[e * 32:e * 32 + 16]
                    t1[yl * 2 + 1, z4 + e] = tt[e * 32 + 16:e * 32 + 32]

    for zz in range(16):
        s[zz, pl.ds(64, 16), :] = t1[j % 4, zz]

    def t_z(t):
        zz = (z + t) % 16
        return remote(s.at[zz], r.at[z], zs.at[t], zr.at[t], (y_lo * 16 + zz, j))

    @pl.loop(0, 15)
    def _(w):
        t_z((16 + (w // 2 + 1) * (1 - 2 * (w % 2))) % 16).start()

    r[z] = s[z]

    @pl.loop(1, 16)
    def _(t):
        remote(b_ref, bl.at[(j - t + 16) % 16], bs.at[t], br.at[t], other).wait_recv()

    pt[...] = lax.dot_general(
        hot[...].astype(BF), bl[...].reshape(128, 1024), NT, preferred_element_type=F32
    ).astype(BF)

    @pl.loop(1, 16)
    def _(t):
        remote(s.at[0], r.at[(z - t + 16) % 16], zs.at[t], zr.at[t], other).wait_recv()

    for zz in range(16):
        rf[pl.ds(zz * 80, 80), :] = r[zz].astype(F32)
    for k in range(80):
        g[k] = rf[pl.ds(k, 16, stride=80), :].astype(BF)

    def rows(yl, jj, shared):
        base = yl * 20 + (16 + jj // 4 if shared else jj)
        return pl.ds(pl.multiple_of(base * 16, 16), 16)

    def t_p(d, dy_lo, dev):
        return remote(g.at[pl.ds(dy_lo * 32, 32)], ta.at[pl.ds(0, 32), rows(y_lo, j, False), :], ps.at[d], pr.at[d], dev)

    def t_q(d, dev):
        return remote(g.at[pl.ds(64, 16)], ta.at[pl.ds((j % 2) * 16, 16), rows(y_lo, j, True), :], qs.at[d], qr.at[d], dev)

    def t_k(d, sv, sj):
        blk = ta.at[pl.ds(0, 32), rows(sv // 16, sj, False), :]
        return remote(blk, blk, ks.at[d], kr.at[d], other)

    def t_l(d, sv, sj):
        blk = ta.at[pl.ds((sj % 2) * 16, 16), rows(sv // 16, sj, True), :]
        return remote(blk, blk, ls.at[d], lr.at[d], other)

    def shared_to(yl, jj):
        return (jj % 4) // 2 == yl

    @pl.loop(1, 16)
    def _(d):
        yy, xx, vv, jj = plane(d, 1)
        t_p(d, yy % 2, (vv, jj)).start()

        @pl.when(shared_to(yy % 2, j))
        def _():
            t_q(d, (vv, jj)).start()

    ta[:, rows(y_lo, j, False), :] = g[pl.ds(y_lo * 32, 32)]
    t_k(0, v, j).start()

    @pl.when(shared_to(y_lo, j))
    def _():
        ta[pl.ds((j % 2) * 16, 16), rows(y_lo, j, True), :] = g[pl.ds(64, 16)]
        t_l(0, v, j).start()

    @pl.loop(1, 16)
    def _(d):
        yy, xx, vv, jj = plane(d, -1)
        remote(g.at[pl.ds(0, 32)], ta.at[pl.ds(0, 32), rows(yy % 2, jj, False), :], ps.at[d], pr.at[d], other).wait_recv()
        t_k(d, vv, jj).start()

        @pl.when(shared_to(y_lo, jj))
        def _():
            remote(g.at[pl.ds(64, 16)], ta.at[pl.ds((jj % 2) * 16, 16), rows(yy % 2, jj, True), :],
                   qs.at[d], qr.at[d], other).wait_recv()
            t_l(d, vv, jj).start()

    @pl.loop(0, 16)
    def _(d):
        yy, xx, vv, jj = plane(d, -1)
        peer = jj + 1 - 2 * core
        t_k(d, vv, peer).wait_recv()

        @pl.when(shared_to(y_lo, peer))
        def _():
            t_l(d, vv, peer).wait_recv()

    @pl.loop(0, 32)
    def _(n):
        part = lax.dot_general(pt[...], ta[n], NT, preferred_element_type=F32)
        for k in range(5):
            hf[k, pl.ds(n, 64, stride=32), :] = part[:, k * 128:(k + 1) * 128]

    @pl.loop(0, 16)
    def _(k):
        part = pl.ds(pl.multiple_of(k * 128, 128), 128)
        for q in range(5):
            h_ref[part, q * 128:(q + 1) * 128] = hf[q, part, :].astype(BF)

    @pl.when(z % 2 == core)
    def _():
        @pl.loop(1, 16)
        def _(t):
            c_z(t).wait_send()

    @pl.loop(1, 16)
    def _(t):
        d_a(t, 0).wait_send()
        d_a(t, 1).wait_send()
        c_p(t, y, x, other).wait_send()
        b_a(t).wait_send()
        t_z(t).wait_send()
        yy, xx, vv, jj = plane(t, 1)
        t_p(t, yy % 2, (vv, jj)).wait_send()

        @pl.when(shared_to(yy % 2, j))
        def _():
            t_q(t, (vv, jj)).wait_send()

    @pl.loop(0, 16)
    def _(d):
        yy, xx, vv, jj = plane(d, -1)
        c_c(d, core, yy, xx).wait_send()
        t_k(d, vv, jj).wait_send()

        @pl.when(shared_to(y_lo, jj))
        def _():
            t_l(d, vv, jj).wait_send()


def shards(density, virt_coeff, block_coeff, ao_order):
    vmem = pl.BlockSpec(memory_space=pltpu.VMEM)
    dma = pltpu.SemaphoreType.DMA
    half, coeff = pl.pallas_call(
        exchange,
        out_shape=(jax.ShapeDtypeStruct((2048, 640), BF), jax.ShapeDtypeStruct((640, 1024), BF)),
        in_specs=[pl.BlockSpec(memory_space=pltpu.SMEM), vmem, vmem, vmem],
        out_specs=(vmem, vmem),
        scratch_shapes=[
            pltpu.VMEM((2, 16, 40, 128), BF),
            pltpu.VMEM((2, 4, 4, 8, 20, 128), BF),
            pltpu.VMEM((16, 8, 1024), BF),
            pltpu.VMEM((64, 1024), F32),
            pltpu.VMEM((64, 128), BF),
            pltpu.VMEM((2, 640, 128), F32),
            pltpu.VMEM((2, 640, 128), BF),
            pltpu.VMEM((32, 24, 128), F32),
            pltpu.VMEM((4, 16, 16, 128), BF),
            pltpu.VMEM((16, 80, 128), BF),
            pltpu.VMEM((16, 80, 128), BF),
            pltpu.VMEM((1280, 128), F32),
            pltpu.VMEM((80, 16, 128), BF),
            pltpu.VMEM((32, 640, 128), BF),
            pltpu.VMEM((5, 2048, 128), F32),
            dma((2, 16)), dma((2, 16)),
            dma((16,)), dma((8,)),
            dma((16,)), dma((16,)),
            dma((16,)), dma((16,)),
            dma((16,)), dma((16,)),
            dma((16,)), dma((16,)),
            dma((16,)), dma((16,)),
            dma((16,)), dma((16,)),
            dma((16,)), dma((16,)),
            dma((16,)), dma((16,)),
        ],
        compiler_params=pltpu.CompilerParams(
            collective_id=0, has_side_effects=True, vmem_limit_bytes=48 * 1024 * 1024
        ),
    )(ao_order, density, virt_coeff, block_coeff)
    out = jnp.dot(half, coeff, preferred_element_type=F32).astype(BF)
    return out.reshape(64, 32, 1024)


def solution(mesh):
    return jax.shard_map(
        shards,
        mesh=mesh,
        in_specs=(P("virt", "ao", None), P("virt", None), P("ao", None), P()),
        out_specs=P("ao", "virt", None),
        check_vma=False,
    )
```

time: 317 us -> 130 us (0.41)
  the two profiles are of different devices: /device:TPU:4 before, /device:TPU:33 now
where the time goes in v1:
time: 130 us
  Pallas kernels  122 us (94%)
  matrix products  4.93 us (4%)
  local copies, waits for them, and re-layouts  3.13 us (2%)
    pallas_call x1, Pallas kernels, shards(): pl.pallas_call(exchange, out_shape=(jax.ShapeDtypeStruct((2048, 640), BF)...  122 us
    dot_general x1, matrix products, shards(): out = jnp.dot(half, coeff, preferred_element_type=F32).astype(BF)  4.93 us
    unnamed x8, local copies, waits for them, and re-layouts  3.13 us

profile of v1, /device:TPU:33, one launch (start us, length us, event | category | flops | bytes accessed | tf_op | source)
XLA Modules:
  0.0 130.0 jit_solution(8844405941472344580)
XLA Ops:
  0.0 0.0 copy-start
  0.0 0.9 copy-done
  0.9 0.0 copy-start.1
  0.9 0.8 copy-done.1
  1.7 0.0 copy-start.2
  1.7 0.7 copy-done.2
  2.4 0.0 copy-start.3
  2.5 0.7 copy-done.3
  3.1 121.9 %shard_map.46 = (bf16[2048,640]{1,0:T(8,128)(2,1)S(1)}, bf16[640,1024]{1,0:T(8,128)(2,1)S(1)}) custom-call(s32[1024]{0:T(1024)S(1)} %copy-done.3, bf16[20,40,128]{2,1,0:T(8,128)(2,1)S(1)} %copy-done, bf16[20,1024]{1,0:T(8,128)(2,1)S(1)} %copy-done.1, bf16[8,1024]{1,0:T(8,128)(2,1)S(1)} %copy-done.2), custom_call_target="tpu_custom_call" | custom-call | tf_op jit(solution)/shard_map/pallas_call | solution.py:301
  125.1 4.9 %convolution_convert_fusion = bf16[2048,1024]{1,0:T(8,128)(2,1)} fusion(bf16[2048,640]{1,0:T(8,128)(2,1)S(1)} %get-tuple-element.7, bf16[640,1024]{1,0:T(8,128)(2,1)S(1)} %get-tuple-element.8), kind=kOutput, calls=%fused_computation | convolution fusion | flops 2686451712 | bytes 8126464 | tf_op jit(solution)/shard_map/dot_general | solution.py:337
Async XLA Ops:
  0.0 0.9 copy-start
  0.9 0.8 copy-start.1
  1.7 0.7 copy-start.2
  2.4 0.7 copy-start.3
